TPU v7x, 768 devices: a whole 4x8x12 slice. The times are simulated.
768 devices in a mesh: dp: 16 (over y, core), shard: 48 (over z, x).
Axes of the slice: x: 4, y: 8, z: 12, core: 2. Of those that a mesh axis runs over, the one named last changes fastest.
Arguments:
- grad: bfloat16 [768, 512, 512], P('shard', 'dp'), may hold values from -150 to 150
- owner: int32 [768], replicated, may hold values from 0 to 47, as said below
- left_root: bfloat16 [48, 32, 512, 512], P('shard', 'dp'), may hold values from -1 to 4
- right_root: bfloat16 [48, 32, 512, 512], P('shard', 'dp'), may hold values from -1 to 4
- momentum: float32 [768, 512, 512], P('shard', 'dp'), may hold values from -6 to 6
Outputs:
- new_momentum: float32 [768, 512, 512], P('shard', 'dp')
Inputs may be any that keep to these rules, and one draw needn't show every extreme that they name: The 16 blocks of one source index (blocks s * 16 to s * 16 + 15) go to distinct owners; no owner index is given more than 32 blocks, and some owner index is given exactly 32 in every draw.
All inputs are finite; a program needn't handle non-finite values.
Results may differ from a plain program's by a relative error of at most 0.017.
Values may be sent and summed in bfloat16 or wider, within the bound.
A program may use at most 32 MiB of HBM per device.

v0:
```python
import jax
import jax.numpy as jnp
from jax import lax
from jax.sharding import PartitionSpec as P

NMAT = 4


EPS = 1e-06
BETA = 0.9


def body(grad, owner, left_root, right_root, momentum):
    n_shard = lax.axis_size("shard")
    blocks, rows, width = grad.shape
    slots = left_root.shape[1]
    most = slots * lax.axis_size("dp")
    nblk = owner.shape[0]
    per_mat = nblk // NMAT
    me_shard = lax.axis_index("shard")
    me_dp = lax.axis_index("dp")
    owners_iota = jnp.arange(n_shard, dtype=jnp.int32)
    block_ids = jnp.arange(nblk, dtype=jnp.int32)
    mat_iota = jnp.arange(NMAT, dtype=jnp.int32)
    hot = (owner[:, None] == owners_iota[None, :]).astype(jnp.int32)
    before = jnp.cumsum(hot, axis=0) - hot
    place = jnp.sum(before * hot, axis=1)
    mine = lax.dynamic_slice_in_dim(owner, me_shard * blocks, blocks)
    route = (owners_iota[:, None] == mine[None, :]).astype(jnp.bfloat16)
    outgoing = jnp.einsum("ok,krc->orc", route, grad, preferred_element_type=jnp.float32).astype(
        jnp.bfloat16
    )
    arrived = lax.all_to_all(outgoing, "shard", split_axis=0, concat_axis=0, tiled=True)
    at_me = owner == me_shard
    select = (place[None, :] == jnp.arange(most, dtype=jnp.int32)[:, None]) & at_me[None, :]
    src_hot = ((block_ids // blocks)[:, None] == owners_iota[None, :]).astype(jnp.float32)
    pick = jnp.dot(select.astype(jnp.float32), src_hot).astype(jnp.bfloat16)
    compact = jnp.einsum("js,src->jrc", pick, arrived, preferred_element_type=jnp.float32).astype(
        jnp.bfloat16
    )
    full = lax.all_to_all(compact, "dp", split_axis=0, concat_axis=1, tiled=True)
    local_sel = lax.dynamic_slice_in_dim(select.astype(jnp.int32), me_dp * slots, slots, 0)
    live = jnp.sum(local_sel, axis=1) > 0
    slot_mats = jnp.sum(local_sel * block_ids[None, :], axis=1) // per_mat
    weight = ((slot_mats[:, None] == mat_iota[None, :]) & live[:, None]).astype(jnp.float32)
    half = jnp.einsum(
        "sij,sjk->sik", full, right_root[0], preferred_element_type=jnp.float32
    ).astype(jnp.bfloat16)
    precond = jnp.einsum("sij,sjk->sik", left_root[0], half, preferred_element_type=jnp.float32)
    pre_terms = jnp.sum(precond * precond, axis=(1, 2))
    full_wide = full.astype(jnp.float32)
    grad_terms = jnp.sum(full_wide * full_wide, axis=(1, 2))
    grad_sq, pre_sq = lax.psum(
        (jnp.dot(grad_terms, weight), jnp.dot(pre_terms, weight)), ("dp", "shard")
    )
    graft = jnp.sqrt(grad_sq / (pre_sq + EPS))
    slot_graft = jnp.dot(weight, graft)
    update = (precond * slot_graft[:, None, None]).astype(jnp.bfloat16)
    rows_back = lax.all_to_all(update, "dp", split_axis=1, concat_axis=0, tiled=True)
    outgoing_back = jnp.einsum(
        "js,jrc->src", pick, rows_back, preferred_element_type=jnp.float32
    ).astype(jnp.bfloat16)
    returned = lax.all_to_all(outgoing_back, "shard", split_axis=0, concat_axis=0, tiled=True)
    landed = jnp.einsum("ok,orc->krc", route, returned, preferred_element_type=jnp.float32)
    return BETA * momentum + landed


def solution(mesh):
    placed = (
        P("shard", "dp", None),
        P(),
        P("shard", "dp", None, None),
        P("shard", "dp", None, None),
        P("shard", "dp", None),
    )
    return jax.shard_map(
        body, mesh=mesh, in_specs=placed, out_specs=P("shard", "dp", None), check_vma=False
    )
```

profile of v0, /device:TPU:1, one launch (start us, length us, event | category | flops | bytes accessed | tf_op | source)
XLA Modules:
  0.0 336.0 jit_solution(17111509471110250342)
XLA Ops:
  0.0 0.0 copy-start
  0.0 0.8 dynamic_slice.6
  0.9 1.7 convolution_convert_fusion
  2.6 2.0 copy.46
  4.6 0.0 copy-start.2
  4.6 19.0 %all-to-all-start = ((bf16[48,32,512]{2,1,0:T(8,128)(2,1)}), bf16[48,32,512]{2,1,0:T(8,128)(2,1)S(1)}, u32[]{:S(2)}, u32[]{:S(2)}) async-start(bf16[48,32,512]{2,1,0:T(8,128)(2,1)} %copy.46), calls=%async_computation | async-start | bytes 3145728 | tf_op jit(solution)/shard_map/all_to_all | solution.py:33
  23.6 0.0 copy-done.2
  23.6 1.8 reduce-window.6
  25.4 0.3 slice_reduce_fusion
  25.7 0.1 fusion.21
  25.8 0.3 fusion.11
  26.1 53.4 %all-to-all-done = bf16[48,32,512]{2,1,0:T(8,128)(2,1)S(1)} async-done(((bf16[48,32,512]{2,1,0:T(8,128)(2,1)}), bf16[48,32,512]{2,1,0:T(8,128)(2,1)S(1)}, u32[]{:S(2)}, u32[]{:S(2)}) %all-to-all-start) | async-done | bytes 1572896 | tf_op jit(solution)/shard_map/all_to_all | solution.py:33
  79.5 1.2 fusion.4
  80.7 1.6 copy.48
  82.2 10.3 %all-to-all-start.1 = ((bf16[32,32,512]{2,1,0:T(8,128)(2,1)}), bf16[32,32,512]{2,1,0:T(8,128)(2,1)S(1)}, u32[]{:S(2)}, u32[]{:S(2)}) async-start(bf16[32,32,512]{2,1,0:T(8,128)(2,1)} %copy.48), calls=%async_computation.1 | async-start | bytes 2097152 | tf_op jit(solution)/shard_map/all_to_all | solution.py:41
  92.6 0.2 multiply_reduce_fusion.2
  92.8 27.7 %all-to-all-done.1 = bf16[32,32,512]{2,1,0:T(8,128)(2,1)S(1)} async-done(((bf16[32,32,512]{2,1,0:T(8,128)(2,1)}), bf16[32,32,512]{2,1,0:T(8,128)(2,1)S(1)}, u32[]{:S(2)}, u32[]{:S(2)}) %all-to-all-start.1) | async-done | bytes 1048608 | tf_op jit(solution)/shard_map/all_to_all | solution.py:41
  120.5 0.4 multiply_reduce_fusion.1
  120.9 0.1 copy.49
  121.0 0.2 convolution_bitcast_fusion.2
  121.2 0.0 copy-done
  121.2 3.8 %multiply_reduce_fusion = (bf16[2]{0:T(256)(128)(2,1)S(1)}, f32[2,512,512]{2,1,0:T(8,128)}) fusion(bf16[1,2,512,512]{3,2,1,0:T(8,128)(2,1)S(1)} %copy-done, bf16[2,512,512]{2,1,0:T(8,128)(2,1)S(1)} %bitcast.70, bf16[1,2,512,512]{3,2,1,0:T(8,128)(2,1)} %param.8), kind=kOutput, calls=%fused_computation.1 | convolution fusion | flops 1075314688 | bytes 5242884 | tf_op jit(solution)/shard_map/sij,sjk->sik/dot_general | solution.py:49
  125.0 0.2 convolution_bitcast_fusion.1
  125.2 104.5 %all-reduce = (f32[4]{0:T(128)S(1)}, f32[4]{0:T(128)S(1)}) all-reduce(f32[4]{0:T(128)S(1)} %convolution_bitcast_fusion.2, f32[4]{0:T(128)S(1)} %convolution_bitcast_fusion.1), channel_id=1, replica_groups=mesh['dp'=16,'shard'=48] {'dp','shard'}, use_global_device_ids=true, to_apply=%region_6.7 | all-reduce | flops 8 | bytes 64 | tf_op jit(solution)/shard_map/psum | solution.py:53
  229.7 0.2 convolution_bitcast_fusion
  229.9 1.9 fusion.12
  231.8 1.0 copy.51
  232.8 34.4 %all_to_all.46 = bf16[2,512,512]{2,0,1:T(2,128)(2,1)S(1)} all-to-all(bf16[2,512,512]{2,0,1:T(2,128)(2,1)S(1)} %copy.51), channel_id=1, replica_groups=mesh['dp'=16,'shard'=48] {'dp'}, dimensions={1} | all-to-all | bytes 2097152 | tf_op jit(solution)/shard_map/all_to_all | solution.py:59
  267.2 0.2 copy.52
  267.4 0.1 copy.53
  267.5 0.9 convolution_convert_fusion.1
  268.4 0.9 copy.55
  269.2 0.0 copy-start.1
  269.2 63.3 %all_to_all.47 = bf16[48,32,512]{2,1,0:T(8,128)(2,1)S(1)} all-to-all(bf16[48,32,512]{2,1,0:T(8,128)(2,1)S(1)} %copy.55), channel_id=1, replica_groups=mesh['dp'=16,'shard'=48] {'shard'}, dimensions={0} | all-to-all | bytes 3145728 | tf_op jit(solution)/shard_map/all_to_all | solution.py:63
  332.5 0.0 copy-done.1
  332.5 1.8 fusion.8
  334.4 1.6 copy.57
  (7 shorter events, 0.1 us)
Async XLA Ops:
  0.0 121.2 %copy-start = (bf16[1,2,512,512]{3,2,1,0:T(8,128)(2,1)S(1)}, bf16[1,2,512,512]{3,2,1,0:T(8,128)(2,1)}, u32[]{:S(2)}) copy-start(bf16[1,2,512,512]{3,2,1,0:T(8,128)(2,1)} %param.7) | copy-start | bytes 3145732
  4.6 19.0 %copy-start.2 = (s32[768]{0:T(1024)S(1)}, s32[768]{0:T(1024)}, u32[]{:S(2)}) copy-start(s32[768]{0:T(1024)} %param.6) | copy-start | bytes 9220
  4.6 74.9 %all-to-all-start = ((bf16[48,32,512]{2,1,0:T(8,128)(2,1)}), bf16[48,32,512]{2,1,0:T(8,128)(2,1)S(1)}, u32[]{:S(2)}, u32[]{:S(2)}) async-start(bf16[48,32,512]{2,1,0:T(8,128)(2,1)} %copy.46), calls=%async_computation | async-start | bytes 3145728 | tf_op jit(solution)/shard_map/all_to_all | solution.py:33
  82.2 38.3 %all-to-all-start.1 = ((bf16[32,32,512]{2,1,0:T(8,128)(2,1)}), bf16[32,32,512]{2,1,0:T(8,128)(2,1)S(1)}, u32[]{:S(2)}, u32[]{:S(2)}) async-start(bf16[32,32,512]{2,1,0:T(8,128)(2,1)} %copy.48), calls=%async_computation.1 | async-start | bytes 2097152 | tf_op jit(solution)/shard_map/all_to_all | solution.py:41
  269.2 63.3 %copy-start.1 = (f32[16,32,512]{2,1,0:T(8,128)S(1)}, f32[16,32,512]{2,1,0:T(8,128)}, u32[]{:S(2)}) copy-start(f32[16,32,512]{2,1,0:T(8,128)} %param.9) | copy-start | bytes 3145732
where the time goes:
time: 336 us
  blocking collectives  202 us (60%)
  waiting for transfers between devices  81.1 us (24%)
  starting transfers between devices  29.3 us (9%)
  matrix products  10.3 us (3%)
  local copies, waits for them, and re-layouts  8.47 us (3%)
  other arithmetic  4.45 us (1%)
    psum x1, blocking collectives, body(): lax.psum((jnp.dot(grad_terms, weight), jnp.dot(pre_terms, weight)), ('dp'...  105 us
    all_to_all x1, blocking collectives, body(): lax.all_to_all(outgoing_back, 'shard', split_axis=0, concat_axis=0, tiled...  63.3 us
    all_to_all x1, waiting for transfers between devices, body(): lax.all_to_all(outgoing, 'shard', split_axis=0, concat_axis=0, tiled=True)  53.4 us
    all_to_all x1, blocking collectives, body(): lax.all_to_all(update, 'dp', split_axis=1, concat_axis=0, tiled=True)  34.4 us
    all_to_all x1, waiting for transfers between devices, body(): lax.all_to_all(compact, 'dp', split_axis=0, concat_axis=1, tiled=True)  27.7 us
    all_to_all x1, starting transfers between devices, body(): lax.all_to_all(outgoing, 'shard', split_axis=0, concat_axis=0, tiled=True)  19 us
    all_to_all x1, starting transfers between devices, body(): lax.all_to_all(compact, 'dp', split_axis=0, concat_axis=1, tiled=True)  10.3 us
  transfers between devices with their start and end apart: 2, of which 2 were waited for; matrix products, arithmetic and copies ran while one was open for 1% of the time, Pallas kernels for 0%

commit v1 on v0

v1 whole, which is shorter than its diff:
```python
import functools

import jax
import jax.numpy as jnp
from jax import lax
from jax.experimental import pallas as pl
from jax.experimental.pallas import tpu as pltpu
from jax.sharding import PartitionSpec as P

NMAT = 4
EPS = 1e-06
BETA = 0.9
LANES = 128
X_RING = 4


def route_tables(owner, n_shard, blocks, most):
    me = lax.axis_index("shard")
    ids = jnp.arange(n_shard, dtype=jnp.int32)
    mine = lax.dynamic_slice_in_dim(owner, me * blocks, blocks)
    ks = jnp.arange(blocks, dtype=jnp.int32)
    block_of = jnp.sum(jnp.where(mine[None, :] == ids[:, None], ks[None, :], 0), axis=1)
    here = jnp.sum((owner.reshape(n_shard, blocks) == me).astype(jnp.int32), axis=1)
    slot_of = jnp.sum(jnp.where(ids[None, :] < ids[:, None], here[None, :], 0), axis=1)
    slots = jnp.arange(most, dtype=jnp.int32)
    hit = (slot_of[None, :] == slots[:, None]) & (here[None, :] > 0)
    source_of = jnp.sum(jnp.where(hit, ids[None, :], 0), axis=1)
    slot_of = jnp.minimum(slot_of, most - 1)
    count = jnp.sum(here, keepdims=True)
    return jnp.concatenate([block_of, source_of, slot_of, mine, count])


def kernel(
    n_dp, n_shard, chunks,
    tab, grad, left_hbm, right_hbm, mom_hbm, out,
    send, pack, full, pre, send2, got, back, got2,
    left, right, mom, acc, half, dp_stat, x_stat, z_stat,
    load_sem, fs_send, fs_recv, fd_send, fd_recv, bd_send, bd_recv, bs_send, bs_recv,
    st_send, st_recv,
):
    blocks, rows, width = grad.shape
    cw = width // chunks
    own = left.shape[0]
    most = own * n_dp
    n_x = X_RING
    n_z = n_shard // n_x
    me_d = lax.axis_index("dp")
    me_s = lax.axis_index("shard")
    me_z = me_s // n_x
    me_x = me_s % n_x
    block_of = lambda o: tab[o]
    source_of = lambda j: tab[n_shard + j]
    slot_of = lambda s: tab[n_shard + most + s]
    owner_of = lambda k: tab[2 * n_shard + most + k]
    live_slots = tab[2 * n_shard + most + blocks]

    loads = [
        pltpu.make_async_copy(src, dst, load_sem.at[i])
        for i, (src, dst) in enumerate(((right_hbm, right), (left_hbm, left), (mom_hbm, mom)))
    ]
    for load in loads:
        load.start()

    barrier = pltpu.get_barrier_semaphore()

    def greet_shard(t, carry):
        pl.semaphore_signal(barrier, inc=1, device_id={"shard": (me_s + t) % n_shard})
        return carry

    def greet_dp(t, carry):
        pl.semaphore_signal(barrier, inc=1, device_id={"dp": (me_d + t) % n_dp})
        return carry

    lax.fori_loop(1, n_shard, greet_shard, 0)
    lax.fori_loop(1, n_dp, greet_dp, 0)

    def fill(o, carry):
        send[o] = grad[block_of(o)]
        return carry

    lax.fori_loop(0, n_shard, fill, 0, unroll=2)

    pl.semaphore_wait(barrier, n_shard - 1 + n_dp - 1)

    def send_shard(src, dst, c, send_sem, recv_sem):
        cols = pl.ds(c * cw, cw)

        def one(t, carry):
            to = (me_s + t) % n_shard
            pltpu.make_async_remote_copy(
                src_ref=src.at[to, :, cols], dst_ref=dst[c].at[me_s],
                send_sem=send_sem.at[c], recv_sem=recv_sem.at[c],
                device_id={"shard": to},
            ).start()
            return carry

        lax.fori_loop(1, n_shard, one, 0)
        dst[c][me_s] = src[me_s, :, c * cw:(c + 1) * cw]

    def wait_bytes(ref, sem):
        pltpu.make_async_copy(ref, ref, sem).wait()

    for c in range(chunks):
        send_shard(send, got, c, fs_send, fs_recv)

    lane = lax.broadcasted_iota(jnp.int32, (1, LANES), 1)
    my_mat = me_s // (n_shard // NMAT)
    wide = grad[...].astype(jnp.float32)
    grad_term = jnp.sum(wide * wide)

    for c in range(chunks):
        wait_bytes(got[c].at[pl.ds(0, n_shard - 1)], fs_recv.at[c])

        def compact(j, carry):
            pack[c, j] = got[c][source_of(j)]
            return carry

        lax.fori_loop(0, most, compact, 0, unroll=4)

        def to_holder(t, carry):
            to = (me_d + t) % n_dp
            pltpu.make_async_remote_copy(
                src_ref=pack.at[c, pl.ds(to * own, own)],
                dst_ref=full.at[c, :, pl.ds(me_d * rows, rows)],
                send_sem=fd_send.at[c], recv_sem=fd_recv.at[c],
                device_id={"dp": to},
            ).start()
            return carry

        lax.fori_loop(1, n_dp, to_holder, 0)
        full[c, :, pl.ds(me_d * rows, rows)] = pack[c, pl.ds(me_d * own, own)]

    loads[0].wait()
    for c in range(chunks):
        wait_bytes(full.at[c, :, pl.ds(0, (n_dp - 1) * rows)], fd_recv.at[c])
        for i in range(own):
            part = jnp.dot(
                full[c, i], right[i, c * cw:(c + 1) * cw, :], preferred_element_type=jnp.float32
            )
            if c > 0:
                part = acc[i] + part
            if c < chunks - 1:
                acc[i] = part
            else:
                half[i] = part.astype(jnp.bfloat16)

    loads[1].wait()
    terms = [jnp.zeros((1, 1), jnp.float32) for _ in range(own)]
    for c in range(chunks):
        for i in range(own):
            part = jnp.dot(
                left[i], half[i, :, c * cw:(c + 1) * cw], preferred_element_type=jnp.float32
            )
            terms[i] += jnp.sum(part * part, keepdims=True)
            pre[c, i] = part.astype(jnp.bfloat16)

        def to_rows(t, carry):
            to = (me_d + t) % n_dp
            pltpu.make_async_remote_copy(
                src_ref=pre.at[c, :, pl.ds(to * rows, rows)],
                dst_ref=back[c].at[pl.ds(me_d * own, own)],
                send_sem=bd_send.at[c], recv_sem=bd_recv.at[c],
                device_id={"dp": to},
            ).start()
            return carry

        lax.fori_loop(1, n_dp, to_rows, 0)
        back[c][pl.ds(me_d * own, own)] = pre[c, :, pl.ds(me_d * rows, rows)]

    stat = jnp.where(lane == my_mat, grad_term, 0.0)
    for i in range(own):
        j = me_d * own + i
        mat = source_of(j) // (n_shard // NMAT)
        stat += jnp.where((lane == NMAT + mat) & (j < live_slots), terms[i], 0.0)

    def share(buf, index, count, which, target):
        def one(t, carry):
            pltpu.make_async_remote_copy(
                src_ref=buf.at[index], dst_ref=buf.at[index],
                send_sem=st_send.at[which], recv_sem=st_recv.at[which],
                device_id=target((index + t) % count),
            ).start()
            return carry

        lax.fori_loop(1, count, one, 0)

    def collect(buf, count, which):
        wait_bytes(buf.at[pl.ds(0, count - 1)], st_recv.at[which])
        return jnp.sum(buf[...], axis=0)

    dp_stat[me_d] = stat
    share(dp_stat, me_d, n_dp, 0, lambda p: {"dp": p})

    for c in range(chunks):
        wait_bytes(back[c].at[pl.ds(0, most - own)], bd_recv.at[c])

        def scatter(s, carry):
            send2[s, :, c * cw:(c + 1) * cw] = back[c][slot_of(s)]
            return carry

        lax.fori_loop(0, n_shard, scatter, 0, unroll=4)
        send_shard(send2, got2, c, bs_send, bs_recv)
        if c == 0:
            x_stat[me_x] = collect(dp_stat, n_dp, 0)
            share(x_stat, me_x, n_x, 1, lambda p: {"shard": me_z * n_x + p})
        if c == chunks - 1:
            z_stat[me_z] = collect(x_stat, n_x, 1)
            share(z_stat, me_z, n_z, 2, lambda p: {"shard": p * n_x + me_x})

    loads[2].wait()
    total = collect(z_stat, n_z, 2)
    grad_sq = jnp.sum(jnp.where(lane == my_mat, total, 0.0), axis=1, keepdims=True)
    pre_sq = jnp.sum(jnp.where(lane == NMAT + my_mat, total, 0.0), axis=1, keepdims=True)
    graft = jnp.sqrt(grad_sq / (pre_sq + EPS))
    for c in range(chunks):
        wait_bytes(got2[c].at[pl.ds(0, n_shard - 1)], bs_recv.at[c])

        def finish(k, carry):
            cols = slice(c * cw, (c + 1) * cw)
            update = graft * got2[c][owner_of(k)].astype(jnp.float32)
            out[k, :, cols] = BETA * mom[k, :, cols] + update
            return carry

        lax.fori_loop(0, blocks, finish, 0, unroll=2)

    for c in range(chunks):
        wait_bytes(send.at[pl.ds(0, n_shard - 1), :, pl.ds(c * cw, cw)], fs_send.at[c])
        wait_bytes(pack.at[c, pl.ds(0, most - own)], fd_send.at[c])
        wait_bytes(pre.at[c, :, pl.ds(0, (n_dp - 1) * rows)], bd_send.at[c])
        wait_bytes(send2.at[pl.ds(0, n_shard - 1), :, pl.ds(c * cw, cw)], bs_send.at[c])
    for which, (buf, count) in enumerate(((dp_stat, n_dp), (x_stat, n_x), (z_stat, n_z))):
        wait_bytes(buf.at[pl.ds(0, count - 1)], st_send.at[which])


def body(grad, owner, left_root, right_root, momentum):
    n_dp, n_shard = lax.axis_size("dp"), lax.axis_size("shard")
    blocks, rows, width = grad.shape
    own = left_root.shape[1]
    most = own * n_dp
    side = left_root.shape[2]
    chunks = max(1, min(4, width // LANES))
    cw = width // chunks
    n_x = X_RING
    n_z = n_shard // n_x
    tab = route_tables(owner, n_shard, blocks, most)
    bf16, f32 = jnp.bfloat16, jnp.float32
    vmem = pl.BlockSpec(memory_space=pltpu.VMEM)
    hbm = pl.BlockSpec(memory_space=pl.ANY)
    dma = pltpu.SemaphoreType.DMA
    flops = 4 * own * side * side * side
    return pl.pallas_call(
        functools.partial(kernel, n_dp, n_shard, chunks),
        out_shape=jax.ShapeDtypeStruct(momentum.shape, f32),
        in_specs=[pl.BlockSpec(memory_space=pltpu.SMEM), vmem, hbm, hbm, hbm],
        out_specs=vmem,
        scratch_shapes=[
            pltpu.VMEM((n_shard, rows, width), bf16),
            pltpu.VMEM((chunks, most, rows, cw), bf16),
            pltpu.VMEM((chunks, own, side, cw), bf16),
            pltpu.VMEM((chunks, own, side, cw), bf16),
            pltpu.VMEM((n_shard, rows, width), bf16),
            [pltpu.VMEM((n_shard, rows, cw), bf16)] * chunks,
            [pltpu.VMEM((most, rows, cw), bf16)] * chunks,
            [pltpu.VMEM((n_shard, rows, cw), bf16)] * chunks,
            pltpu.VMEM((own, side, width), bf16),
            pltpu.VMEM((own, side, width), bf16),
            pltpu.VMEM(momentum.shape, f32),
            pltpu.VMEM((own, side, width), f32),
            pltpu.VMEM((own, side, width), bf16),
            pltpu.VMEM((n_dp, 1, LANES), f32),
            pltpu.VMEM((n_x, 1, LANES), f32),
            pltpu.VMEM((n_z, 1, LANES), f32),
            dma((3,)),
            dma((chunks,)), dma((chunks,)), dma((chunks,)), dma((chunks,)),
            dma((chunks,)), dma((chunks,)), dma((chunks,)), dma((chunks,)),
            dma((3,)), dma((3,)),
        ],
        compiler_params=pltpu.CompilerParams(
            collective_id=0, has_side_effects=True, vmem_limit_bytes=56 * 1024 * 1024
        ),
        cost_estimate=pl.CostEstimate(flops=flops, bytes_accessed=5 << 20, transcendentals=0),
    )(tab, grad, left_root[0], right_root[0], momentum)


def solution(mesh):
    placed = (
        P("shard", "dp", None),
        P(),
        P("shard", "dp", None, None),
        P("shard", "dp", None, None),
        P("shard", "dp", None),
    )
    return jax.shard_map(
        body, mesh=mesh, in_specs=placed, out_specs=P("shard", "dp", None), check_vma=False
    )
```

time: 336 us -> 160 us (0.48)
  blocking collectives: 202 us -> 0 us
  Pallas kernels: 0 us -> 154 us
  waiting for transfers between devices: 81.1 us -> 0 us
  starting transfers between devices: 29.3 us -> 0 us
  matrix products: 10.3 us -> 0 us
  local copies, waits for them, and re-layouts: 8.47 us -> 4.46 us
    pallas_call x0 -> x1, Pallas kernels: none -> 154 us  [body(): pl.pallas_call(functools.partial(kernel, n_dp, n_shard, chunks), out_shap...]
    psum x1 -> x0, blocking collectives: 105 us -> none  [body(): lax.psum((jnp.dot(grad_terms, weight), jnp.dot(pre_terms, weight)), ('dp'...]
    all_to_all x2 -> x0, blocking collectives: 97.7 us -> none  [the longest x1 63.3 us: body(): lax.all_to_all(outgoing_back, 'shard', split_axis=0, concat_axis=0, tiled...]
    all_to_all x2 -> x0, waiting for transfers between devices: 81.1 us -> none  [the longest x1 53.4 us: body(): lax.all_to_all(outgoing, 'shard', split_axis=0, concat_axis=0, tiled=True)]
    all_to_all x2 -> x0, starting transfers between devices: 29.3 us -> none  [the longest x1 19 us: body(): lax.all_to_all(outgoing, 'shard', split_axis=0, concat_axis=0, tiled=True)]
    dot_general x9 -> x0, matrix products: 10.3 us -> none  [the longest x1 3.84 us: body(): jnp.einsum('sij,sjk->sik', left_root[0], half, preferred_element_type=jnp...]
    convert_element_type x4 -> x1, local copies, waits for them, and re-layouts: 5.42 us -> 0.07 us  [route_tables(): (owner.reshape(n_shard, blocks) == me).astype(jnp.int32)]
  transfers between devices with their start and end apart: 2 -> 0, of which waited for: 2 -> 0; matrix products, arithmetic and copies ran while one was open for 1% -> 0% of each run, Pallas kernels for 0% -> 0%
where the time goes in v1:
time: 160 us
  Pallas kernels  154 us (96%)
  local copies, waits for them, and re-layouts  4.46 us (3%)
    pallas_call x1, Pallas kernels, body(): pl.pallas_call(functools.partial(kernel, n_dp, n_shard, chunks), out_shap...  154 us

profile of v1, /device:TPU:1, one launch (start us, length us, event | category | flops | bytes accessed | tf_op | source)
XLA Modules:
  0.0 159.6 jit_solution(3654609707515123729)
XLA Ops:
  0.0 0.0 copy-start
  0.0 0.7 copy-done
  0.7 0.1 dynamic_slice.3
  0.8 0.1 select_reduce_fusion.2
  0.9 0.7 fusion.1
  1.6 0.1 reshape.12
  1.6 0.1 reduce_sum.46
  1.8 0.1 select_reduce_fusion
  1.9 0.1 select_reduce_fusion.1
  2.0 1.3 concatenate.3.tab
  3.3 153.9 %shard_map.55 = f32[16,32,512]{2,1,0:T(8,128)} custom-call(s32[145]{0:T(256)} %concatenate.3.tab, bf16[16,32,512]{2,1,0:T(8,128)(2,1)} %grad.1, bf16[2,512,512]{2,1,0:T(8,128)(2,1)} %bitcast.3, bf16[2,512,512]{2,1,0:T(8,128)(2,1)} %bitcast.4, f32[16,32,512]{2,1,0:T(8,128)} %mom_hbm.1), custom_call_target="tpu_custom_call" | custom-call | flops 1073741824 | bytes 5242880 | tf_op jit(solution)/shard_map/pallas_call | solution.py:251
  157.3 2.3 %copy.7 = f32[16,32,512]{2,1,0:T(8,128)} copy(f32[16,32,512]{2,1,0:T(8,128)} %shard_map.55) | data formatting | bytes 2097152
  (2 shorter events, 0.0 us)
Async XLA Ops:
  0.0 0.7 copy-start

commit v2 on v1

v2 whole, which is shorter than its diff:
```python
import functools

import jax
import jax.numpy as jnp
from jax import lax
from jax.experimental import pallas as pl
from jax.experimental.pallas import tpu as pltpu
from jax.sharding import PartitionSpec as P

NMAT = 4
EPS = 1e-06
BETA = 0.9
LANES = 128
VMEM_LIMIT = 53 << 20
UNROLL_SEND = 1
UNROLL_MOVE = 2
X_RING = 4


def route_tables(owner, n_shard, blocks, most):
    me = lax.axis_index("shard")
    ids = jnp.arange(n_shard, dtype=jnp.int32)
    mine = lax.dynamic_slice_in_dim(owner, me * blocks, blocks)
    ks = jnp.arange(blocks, dtype=jnp.int32)
    block_of = jnp.sum(jnp.where(mine[None, :] == ids[:, None], ks[None, :], 0), axis=1)
    here = jnp.sum((owner.reshape(n_shard, blocks) == me).astype(jnp.int32), axis=1)
    slot_of = jnp.sum(jnp.where(ids[None, :] < ids[:, None], here[None, :], 0), axis=1)
    slots = jnp.arange(most, dtype=jnp.int32)
    hit = (slot_of[None, :] == slots[:, None]) & (here[None, :] > 0)
    source_of = jnp.sum(jnp.where(hit, ids[None, :], 0), axis=1)
    slot_of = jnp.minimum(slot_of, most - 1)
    count = jnp.sum(here, keepdims=True)
    return jnp.concatenate([block_of, source_of, slot_of, mine, count])


def kernel(
    n_dp, n_shard, spans_out, spans_back, parts_out, parts_back,
    tab, grad_hbm, left_hbm, right_hbm, update,
    grad, send, pack, full, pre, send2, got, back, got2,
    left, right, acc, half, dp_stat, x_stat, z_stat,
    load_sem, fs_send, fs_recv, fd_send, fd_recv, bd_send, bd_recv, bs_send, bs_recv,
    st_send, st_recv,
):
    blocks, rows, width = grad.shape
    own = left.shape[0]
    most = own * n_dp
    n_x = X_RING
    n_z = n_shard // n_x
    me_d = lax.axis_index("dp")
    me_s = lax.axis_index("shard")
    me_z = me_s // n_x
    me_x = me_s % n_x
    block_of = lambda o: tab[o]
    source_of = lambda j: tab[n_shard + j]
    slot_of = lambda s: tab[n_shard + most + s]
    owner_of = lambda k: tab[2 * n_shard + most + k]
    live_slots = tab[2 * n_shard + most + blocks]

    loads = [
        pltpu.make_async_copy(src, dst, load_sem.at[i])
        for i, (src, dst) in enumerate(((grad_hbm, grad), (right_hbm, right), (left_hbm, left)))
    ]
    for load in loads:
        load.start()

    barrier = pltpu.get_barrier_semaphore()

    def greet_shard(t, carry):
        pl.semaphore_signal(barrier, inc=1, device_id={"shard": (me_s + t) % n_shard})
        return carry

    def greet_dp(t, carry):
        pl.semaphore_signal(barrier, inc=1, device_id={"dp": (me_d + t) % n_dp})
        return carry

    lax.fori_loop(1, n_shard, greet_shard, 0)
    lax.fori_loop(1, n_dp, greet_dp, 0)

    loads[0].wait()

    def fill(o, carry):
        send[o] = grad[block_of(o)]
        return carry

    lax.fori_loop(0, n_shard, fill, 0, unroll=UNROLL_MOVE)

    pl.semaphore_wait(barrier, n_shard - 1 + n_dp - 1)

    def wait_bytes(ref, sem):
        pltpu.make_async_copy(ref, ref, sem).wait()

    def send_shard(src, dst, p, part, send_sem, recv_sem):
        span, r0, nr = part

        def one(t, carry):
            to = (me_s + t) % n_shard
            pltpu.make_async_remote_copy(
                src_ref=src.at[to, pl.ds(r0, nr), pl.ds(*span)], dst_ref=dst[p].at[me_s],
                send_sem=send_sem.at[p], recv_sem=recv_sem.at[p],
                device_id={"shard": to},
            ).start()
            return carry

        lax.fori_loop(1, n_shard, one, 0, unroll=UNROLL_SEND)
        dst[p][me_s] = src[me_s, r0:r0 + nr, pl.ds(*span)]

    for p, part in enumerate(parts_out):
        send_shard(send, got, p, part, fs_send, fs_recv)

    lane = lax.broadcasted_iota(jnp.int32, (1, LANES), 1)
    my_mat = me_s // (n_shard // NMAT)
    wide = grad[...].astype(jnp.float32)
    grad_term = jnp.sum(wide * wide)

    p_of = {span: i for i, span in enumerate(spans_out)}

    for p, (span, r0, nr) in enumerate(parts_out):
        wait_bytes(got[p].at[pl.ds(0, n_shard - 1)], fs_recv.at[p])

        def compact(j, carry):
            pack[j, r0:r0 + nr, pl.ds(*span)] = got[p][source_of(j)]
            return carry

        lax.fori_loop(0, most, compact, 0, unroll=UNROLL_MOVE)

        def to_holder(t, carry):
            to = (me_d + t) % n_dp
            pltpu.make_async_remote_copy(
                src_ref=pack.at[pl.ds(to * own, own), pl.ds(r0, nr), pl.ds(*span)],
                dst_ref=full[p_of[span]].at[:, pl.ds(me_d * rows + r0, nr)],
                send_sem=fd_send.at[p], recv_sem=fd_recv.at[p],
                device_id={"dp": to},
            ).start()
            return carry

        lax.fori_loop(1, n_dp, to_holder, 0, unroll=UNROLL_SEND)
        full[p_of[span]][:, pl.ds(me_d * rows + r0, nr)] = pack[
            pl.ds(me_d * own, own), r0:r0 + nr, pl.ds(*span)
        ]

    loads[1].wait()
    for c, span in enumerate(spans_out):
        for p, part in enumerate(parts_out):
            if part[0] == span:
                wait_bytes(full[c].at[:, pl.ds(0, (n_dp - 1) * part[2])], fd_recv.at[p])
        for i in range(own):
            term = jnp.dot(
                full[c][i], right[i, pl.ds(*span), :], preferred_element_type=jnp.float32
            )
            if c > 0:
                term = acc[i] + term
            if c < len(spans_out) - 1:
                acc[i] = term
            else:
                half[i] = term.astype(jnp.bfloat16)

    loads[2].wait()
    terms = [jnp.zeros((1, 1), jnp.float32) for _ in range(own)]

    def precondition(span):
        for i in range(own):
            term = jnp.dot(
                left[i], half[i, :, pl.ds(*span)], preferred_element_type=jnp.float32
            )
            terms[i] += jnp.sum(term * term, keepdims=True)
            pre[i, :, pl.ds(*span)] = term.astype(jnp.bfloat16)

    def send_rows(p):
        span, r0, nr = parts_back[p]

        def one(t, carry):
            to = (me_d + t) % n_dp
            pltpu.make_async_remote_copy(
                src_ref=pre.at[:, pl.ds(to * rows + r0, nr), pl.ds(*span)],
                dst_ref=back[p].at[pl.ds(me_d * own, own)],
                send_sem=bd_send.at[p], recv_sem=bd_recv.at[p],
                device_id={"dp": to},
            ).start()
            return carry

        lax.fori_loop(1, n_dp, one, 0, unroll=UNROLL_SEND)
        back[p][pl.ds(me_d * own, own)] = pre[
            :, pl.ds(me_d * rows + r0, nr), pl.ds(*span)
        ]

    def share(buf, index, count, which, target):
        def one(t, carry):
            pltpu.make_async_remote_copy(
                src_ref=buf.at[index], dst_ref=buf.at[index],
                send_sem=st_send.at[which], recv_sem=st_recv.at[which],
                device_id=target((index + t) % count),
            ).start()
            return carry

        lax.fori_loop(1, count, one, 0)

    def collect(buf, count, which):
        wait_bytes(buf.at[pl.ds(0, count - 1)], st_recv.at[which])
        return jnp.sum(buf[...], axis=0)

    precondition(spans_back[0])
    for p, part in enumerate(parts_back):
        if part[0] == spans_back[0]:
            send_rows(p)
    for span in spans_back[1:]:
        precondition(span)
    stat = jnp.where(lane == my_mat, grad_term, 0.0)
    for i in range(own):
        mat = source_of(me_d * own + i) // (n_shard // NMAT)
        stat += jnp.where((lane == NMAT + mat) & (me_d * own + i < live_slots), terms[i], 0.0)
    dp_stat[me_d] = stat
    share(dp_stat, me_d, n_dp, 0, lambda p: {"dp": p})
    for p, part in enumerate(parts_back):
        if part[0] != spans_back[0]:
            send_rows(p)

    last = len(parts_back) - 1
    for p, (span, r0, nr) in enumerate(parts_back):
        if p == last:
            z_stat[me_z] = collect(x_stat, n_x, 1)
            share(z_stat, me_z, n_z, 2, lambda p: {"shard": p * n_x + me_x})
        wait_bytes(back[p].at[pl.ds(0, most - own)], bd_recv.at[p])

        def scatter(s, carry):
            send2[s, r0:r0 + nr, pl.ds(*span)] = back[p][slot_of(s)]
            return carry

        lax.fori_loop(0, n_shard, scatter, 0, unroll=UNROLL_MOVE)
        send_shard(send2, got2, p, parts_back[p], bs_send, bs_recv)
        if p == max(0, last - 2):
            x_stat[me_x] = collect(dp_stat, n_dp, 0)
            share(x_stat, me_x, n_x, 1, lambda p: {"shard": me_z * n_x + p})

    total = collect(z_stat, n_z, 2)
    grad_sq = jnp.sum(jnp.where(lane == my_mat, total, 0.0), axis=1, keepdims=True)
    pre_sq = jnp.sum(jnp.where(lane == NMAT + my_mat, total, 0.0), axis=1, keepdims=True)
    graft = jnp.sqrt(grad_sq / (pre_sq + EPS))
    for p, (span, r0, nr) in enumerate(parts_back):
        wait_bytes(got2[p].at[pl.ds(0, n_shard - 1)], bs_recv.at[p])

        def finish(k, carry):
            scaled = graft * got2[p][owner_of(k)].astype(jnp.float32)
            update[k, r0:r0 + nr, pl.ds(*span)] = scaled.astype(jnp.bfloat16)
            return carry

        lax.fori_loop(0, blocks, finish, 0, unroll=UNROLL_MOVE)

    for p, (span, r0, nr) in enumerate(parts_out):
        area = pl.ds(r0, nr), pl.ds(*span)
        wait_bytes(send.at[(pl.ds(0, n_shard - 1), *area)], fs_send.at[p])
        wait_bytes(pack.at[(pl.ds(0, most - own), *area)], fd_send.at[p])
    for p, (span, r0, nr) in enumerate(parts_back):
        area = pl.ds(r0, nr), pl.ds(*span)
        wait_bytes(pre.at[:, pl.ds(0, (n_dp - 1) * nr), pl.ds(*span)], bd_send.at[p])
        wait_bytes(send2.at[(pl.ds(0, n_shard - 1), *area)], bs_send.at[p])
    for which, (buf, count) in enumerate(((dp_stat, n_dp), (x_stat, n_x), (z_stat, n_z))):
        wait_bytes(buf.at[pl.ds(0, count - 1)], st_send.at[which])


def body(grad, owner, left_root, right_root, momentum):
    n_dp, n_shard = lax.axis_size("dp"), lax.axis_size("shard")
    blocks, rows, width = grad.shape
    own = left_root.shape[1]
    most = own * n_dp
    side = left_root.shape[2]
    n_x = X_RING
    n_z = n_shard // n_x
    halves = ((0, rows // 2), (rows // 2, rows // 2))
    big = width - 2 * LANES
    spans_out = [(0, big)] if big else []
    spans_out += [(big, LANES), (big + LANES, LANES)]
    spans_back = [(0, LANES), (LANES, LANES)] + ([(2 * LANES, big)] if big else [])
    parts_out = [(span, 0, rows) for span in spans_out[:-1]]
    parts_out += [(spans_out[-1], *h) for h in halves]
    parts_back = [(spans_back[0], *h) for h in halves]
    parts_back += [(span, 0, rows) for span in spans_back[1:]]
    n_out, n_back = len(parts_out), len(parts_back)
    tab = route_tables(owner, n_shard, blocks, most)
    bf16, f32 = jnp.bfloat16, jnp.float32
    vmem = pl.BlockSpec(memory_space=pltpu.VMEM)
    hbm = pl.BlockSpec(memory_space=pl.ANY)
    dma = pltpu.SemaphoreType.DMA
    flops = 4 * own * side * side * side
    update = pl.pallas_call(
        functools.partial(kernel, n_dp, n_shard, spans_out, spans_back, parts_out, parts_back),
        out_shape=jax.ShapeDtypeStruct(grad.shape, bf16),
        in_specs=[pl.BlockSpec(memory_space=pltpu.SMEM), hbm, hbm, hbm],
        out_specs=vmem,
        scratch_shapes=[
            pltpu.VMEM(grad.shape, bf16),
            pltpu.VMEM((n_shard, rows, width), bf16),
            pltpu.VMEM((most, rows, width), bf16),
            [pltpu.VMEM((own, side, w), bf16) for _, w in spans_out],
            pltpu.VMEM((own, side, width), bf16),
            pltpu.VMEM((n_shard, rows, width), bf16),
            [pltpu.VMEM((n_shard, nr, span[1]), bf16) for span, _, nr in parts_out],
            [pltpu.VMEM((most, nr, span[1]), bf16) for span, _, nr in parts_back],
            [pltpu.VMEM((n_shard, nr, span[1]), bf16) for span, _, nr in parts_back],
            pltpu.VMEM((own, side, width), bf16),
            pltpu.VMEM((own, side, width), bf16),
            pltpu.VMEM((own, side, width), f32),
            pltpu.VMEM((own, side, width), bf16),
            pltpu.VMEM((n_dp, 1, LANES), f32),
            pltpu.VMEM((n_x, 1, LANES), f32),
            pltpu.VMEM((n_z, 1, LANES), f32),
            dma((3,)),
            dma((n_out,)), dma((n_out,)), dma((n_out,)), dma((n_out,)),
            dma((n_back,)), dma((n_back,)), dma((n_back,)), dma((n_back,)),
            dma((3,)), dma((3,)),
        ],
        compiler_params=pltpu.CompilerParams(
            collective_id=0, has_side_effects=True, vmem_limit_bytes=VMEM_LIMIT
        ),
        cost_estimate=pl.CostEstimate(flops=flops, bytes_accessed=5 << 20, transcendentals=0),
    )(tab, grad, left_root[0], right_root[0])
    return BETA * momentum + update.astype(f32)


def solution(mesh):
    placed = (
        P("shard", "dp", None),
        P(),
        P("shard", "dp", None, None),
        P("shard", "dp", None, None),
        P("shard", "dp", None),
    )
    return jax.shard_map(
        body, mesh=mesh, in_specs=placed, out_specs=P("shard", "dp", None), check_vma=False
    )
```

time: 160 us -> 149 us (0.931); the launches traced: 160 us -> 146 us
  Pallas kernels: 154 us -> 142 us
  local copies, waits for them, and re-layouts: 4.46 us -> 1.56 us
    pallas_call x1, Pallas kernels: 154 us -> 142 us  [body(): pl.pallas_call(functools.partial(kernel, n_dp, n_shard, spans_out, spans_...]
    unnamed x3 -> x4, local copies, waits for them, and re-layouts: 2.97 us -> 0.69 us
where the time goes in v2:
time: 149 us; the launch traced here: 146 us
  Pallas kernels  142 us (95%)
  other arithmetic  2.22 us (1%)
  local copies, waits for them, and re-layouts  1.56 us (1%)
    pallas_call x1, Pallas kernels, body(): pl.pallas_call(functools.partial(kernel, n_dp, n_shard, spans_out, spans_...  142 us

profile of v2, /device:TPU:1, one launch (start us, length us, event | category | flops | bytes accessed | tf_op | source)
XLA Modules:
  0.0 146.0 jit_solution(14116101324175923915)
XLA Ops:
  0.0 0.0 copy-start.1
  0.0 0.7 copy-done.1
  0.7 0.1 dynamic_slice.3
  0.8 0.1 select_reduce_fusion.2
  0.9 0.6 fusion.1
  1.5 0.1 reshape.12
  1.6 0.1 reduce_sum.46
  1.7 0.1 select_reduce_fusion
  1.8 0.1 select_reduce_fusion.1
  1.9 0.7 concatenate.3.tab
  2.7 0.0 copy-start
  2.7 142.2 %shard_map.55 = bf16[16,32,512]{2,1,0:T(8,128)(2,1)S(1)} custom-call(s32[145]{0:T(256)S(1)} %concatenate.3.tab, bf16[16,32,512]{2,1,0:T(8,128)(2,1)} %grad_hbm.1, bf16[2,512,512]{2,1,0:T(8,128)(2,1)} %bitcast.3, bf16[2,512,512]{2,1,0:T(8,128)(2,1)} %bitcast.4), custom_call_target="tpu_custom_call" | custom-call | flops 1073741824 | bytes 5242880 | tf_op jit(solution)/shard_map/pallas_call | solution.py:284
  144.8 0.0 copy-done
  144.9 1.2 convert_add_fusion
  (2 shorter events, 0.0 us)
Async XLA Ops:
  0.0 0.7 copy-start.1
  2.7 142.2 %copy-start = (f32[16,32,512]{2,1,0:T(8,128)S(1)}, f32[16,32,512]{2,1,0:T(8,128)}, u32[]{:S(2)}) copy-start(f32[16,32,512]{2,1,0:T(8,128)} %param.9) | copy-start | bytes 3145732

commit v3 on v2

--- a/solution.py
+++ b/solution.py
@@ -93,7 +93,10 @@
         span, r0, nr = part
 
         def one(t, carry):
-            to = (me_s + t) % n_shard
+            u = n_shard - t
+            hop = u // n_x
+            dz = ((hop + 1) // 2) * (2 * (hop % 2) - 1)
+            to = (me_z + dz + n_z) % n_z * n_x + (me_x + u) % n_x
             pltpu.make_async_remote_copy(
                 src_ref=src.at[to, pl.ds(r0, nr), pl.ds(*span)], dst_ref=dst[p].at[me_s],
                 send_sem=send_sem.at[p], recv_sem=recv_sem.at[p],

time: 149 us -> 147 us (0.987); the launches traced: 146 us -> 147 us
  no operation moved by 1% of the time
where the time goes in v3:
time: 147 us
  Pallas kernels  143 us (97%)
  other arithmetic  2.22 us (2%)
  local copies, waits for them, and re-layouts  1.56 us (1%)
    pallas_call x1, Pallas kernels, body(): pl.pallas_call(functools.partial(kernel, n_dp, n_shard, spans_out, spans_...  143 us

profile of v3, /device:TPU:1, one launch (start us, length us, event | category | flops | bytes accessed | tf_op | source)
XLA Modules:
  0.0 146.6 jit_solution(5997248728482248556)
XLA Ops:
  0.0 0.0 copy-start.1
  0.0 0.7 copy-done.1
  0.7 0.1 dynamic_slice.3
  0.8 0.1 select_reduce_fusion.2
  0.9 0.6 fusion.1
  1.5 0.1 reshape.12
  1.6 0.1 reduce_sum.46
  1.7 0.1 select_reduce_fusion
  1.8 0.1 select_reduce_fusion.1
  1.9 0.7 concatenate.3.tab
  2.7 0.0 copy-start
  2.7 142.7 %shard_map.55 = bf16[16,32,512]{2,1,0:T(8,128)(2,1)S(1)} custom-call(s32[145]{0:T(256)S(1)} %concatenate.3.tab, bf16[16,32,512]{2,1,0:T(8,128)(2,1)} %grad_hbm.1, bf16[2,512,512]{2,1,0:T(8,128)(2,1)} %bitcast.3, bf16[2,512,512]{2,1,0:T(8,128)(2,1)} %bitcast.4), custom_call_target="tpu_custom_call" | custom-call | flops 1073741824 | bytes 5242880 | tf_op jit(solution)/shard_map/pallas_call | solution.py:287
  145.4 0.0 copy-done
  145.4 1.2 convert_add_fusion
  (2 shorter events, 0.0 us)
Async XLA Ops:
  0.0 0.7 copy-start.1
  2.7 142.8 %copy-start = (f32[16,32,512]{2,1,0:T(8,128)S(1)}, f32[16,32,512]{2,1,0:T(8,128)}, u32[]{:S(2)}) copy-start(f32[16,32,512]{2,1,0:T(8,128)} %param.9) | copy-start | bytes 3145732
